TPU v7x, 32 devices: a whole 2x2x4 slice. The times are simulated.
32 devices in a mesh: lat: 8 (over y, x, core), lon: 4 (over z).
Axes of the slice: x: 2, y: 2, z: 4, core: 2. Of those that a mesh axis runs over, the one named last changes fastest.
Arguments:
- grid_state: bfloat16 [384, 768, 128], P('lat', 'lon'), may hold values from -6 to 6
- upstream: bfloat16 [384, 768, 128], P('lat', 'lon'), may hold values from -6 to 6
- spectral_weight: bfloat16 [128, 384, 2, 128], P('lon', 'lat'), may hold values from -0.375 to 0.375
- up_weight: bfloat16 [128, 512], replicated, may hold values from -0.5 to 0.5
- down_weight: bfloat16 [512, 128], replicated, may hold values from -0.25 to 0.25
Outputs:
- next_state: bfloat16 [384, 768, 128], P('lat', 'lon')
- grad_state: bfloat16 [384, 768, 128], P('lat', 'lon')
- grad_spectral: float32 [128, 384, 2, 128], P('lon', 'lat')
- grad_up: float32 [128, 512], replicated
- grad_down: float32 [512, 128], replicated
All inputs are finite; a program needn't handle non-finite values.
Results may differ from a plain program's by a relative error of at most 0.02.
Values may be sent and summed in bfloat16 or wider, within the bound.
A program may use at most 256 MiB of HBM per device.

v0:
```python
import jax
import jax.numpy as jnp
import numpy as np
from jax import lax
from jax.sharding import PartitionSpec as P


def fourier_tables(lon_cells, order_ids):
    cell_ids = np.arange(lon_cells)
    phase_ids = cell_ids[:, None] * order_ids[None, :] % lon_cells
    angles = 2.0 * np.pi * phase_ids / lon_cells
    unit_scale = 2.0 * np.pi / lon_cells
    forward = np.stack([np.cos(angles) * unit_scale, -np.sin(angles) * unit_scale], axis=1)
    factor = np.where(order_ids == 0, 1.0, 2.0)[:, None]
    inverse = np.stack([np.cos(angles).T * factor, -np.sin(angles).T * factor], axis=0)
    return (forward, inverse)


def latitude_tables(lat_cells):
    cycle_ids = np.arange(lat_cells)
    colatitude = np.pi * (cycle_ids + 0.5) / lat_cells
    harmonics = np.arange(1, lat_cells // 2 + 1)
    series = np.cos(2.0 * harmonics[None, :] * colatitude[:, None]) / (
        4.0 * harmonics[None, :] * harmonics[None, :] - 1.0
    )
    quad = 2.0 / lat_cells * (1.0 - 2.0 * np.sum(series, axis=1))
    return (np.cos(colatitude), np.log(np.sin(colatitude)), quad)


def diagonal_logs(order_count):
    order_ids = np.arange(1, order_count)
    log_steps = 0.5 * np.log((2.0 * order_ids + 1.0) / (2.0 * order_ids))
    return np.concatenate([np.zeros(1), np.cumsum(log_steps)]) - 0.5 * np.log(4.0 * np.pi)


def legendre_step(carry_state, degree, orders_col, cos_row, start_logs):
    newest, former, logscale = carry_state
    degree_f = degree.astype(jnp.float32)
    is_below = degree_f < orders_col
    is_diag = degree_f == orders_col
    is_above = degree_f > orders_col
    square = orders_col * orders_col
    grow_coef = jnp.sqrt(
        (4.0 * degree_f * degree_f - 1.0) / jnp.maximum(degree_f * degree_f - square, 1.0)
    )
    lagged = degree_f - 1.0
    shrink = jnp.sqrt(
        jnp.maximum(lagged * lagged - square, 0.0) / jnp.maximum(4.0 * lagged * lagged - 1.0, 1.0)
    )
    new_value = jnp.where(
        is_above, grow_coef * (cos_row * newest - shrink * former), jnp.where(is_diag, 1.0, 0.0)
    )
    logscale = jnp.where(is_diag, start_logs, logscale)
    former = newest
    newest = new_value
    rescale = jnp.where(is_below, 1.0, jnp.maximum(jnp.abs(newest), jnp.abs(former)))
    newest = newest / rescale
    former = former / rescale
    logscale = logscale + jnp.log(rescale)
    return ((newest, former, logscale), newest * jnp.exp(logscale))


def legendre_tables(orders_col, start_logs, cos_row, quad_row, degrees):
    unroll = 16
    zeros_state = jnp.zeros((orders_col.shape[0], cos_row.shape[1]), jnp.float32)

    def advance(carry_state, opening):
        collected = []
        for offset in range(unroll):
            carry_state, new_value = legendre_step(
                carry_state, opening + offset, orders_col, cos_row, start_logs
            )
            collected.append(new_value)
        stacked = jnp.stack(collected)
        return (
            carry_state,
            (stacked.astype(jnp.bfloat16), (stacked * quad_row).astype(jnp.bfloat16)),
        )

    openings = jnp.arange(0, degrees, unroll, dtype=jnp.int32)
    final_state, (plain, weighted) = lax.scan(
        advance, (zeros_state, zeros_state, zeros_state), openings
    )
    full_shape = (degrees, orders_col.shape[0], cos_row.shape[1])
    return (plain.reshape(full_shape), weighted.reshape(full_shape))


def order_slots(degrees):
    slot_ids = np.arange(degrees)
    return slot_ids


def degree_blocks(degrees, per_device):
    return [(0, degrees, per_device)]


def to_degrees(cycle_input, basis_table, blocks):
    order_total = cycle_input.shape[2]
    pieces_list = []
    for opening, block_size, needed in blocks:
        block_part = jnp.einsum(
            "lkj,jrkc->lrkc",
            basis_table[opening : opening + block_size, :needed],
            cycle_input[:, :, :needed],
            preferred_element_type=jnp.float32,
        )
        if needed < order_total:
            block_part = jnp.pad(block_part, ((0, 0), (0, 0), (0, order_total - needed), (0, 0)))
        pieces_list.append(block_part)
    return jnp.concatenate(pieces_list, axis=0).astype(jnp.bfloat16)


def to_latitudes(degree_input, basis_table, blocks):
    order_total = degree_input.shape[2]
    accum = None
    for opening, block_size, needed in blocks:
        block_part = jnp.einsum(
            "lkj,lrkc->jrkc",
            basis_table[opening : opening + block_size, :needed],
            degree_input[opening : opening + block_size, :, :needed],
            preferred_element_type=jnp.float32,
        )
        if needed < order_total:
            block_part = jnp.pad(block_part, ((0, 0), (0, 0), (0, order_total - needed), (0, 0)))
        accum = block_part
    return accum.astype(jnp.bfloat16)


def grid_to_orders(grid_values, fourier_table, letters):
    spectrum = jnp.einsum(
        letters,
        lax.all_to_all(grid_values, "lon", split_axis=2, concat_axis=1, tiled=True),
        fourier_table,
        preferred_element_type=jnp.float32,
    ).astype(jnp.bfloat16)
    return lax.all_to_all(spectrum, "lon", split_axis=2, concat_axis=3, tiled=True)


def orders_to_grid(order_values, fourier_table, letters):
    columns = jnp.einsum(
        letters,
        lax.all_to_all(order_values, "lon", split_axis=3, concat_axis=2, tiled=True),
        fourier_table,
        preferred_element_type=jnp.float32,
    ).astype(jnp.bfloat16)
    return lax.all_to_all(columns, "lon", split_axis=1, concat_axis=2, tiled=True)


def to_spectral(order_values, basis_table, blocks):
    cycle_input = lax.all_to_all(order_values, "lat", split_axis=3, concat_axis=0, tiled=True)
    degree_values = to_degrees(cycle_input, basis_table, blocks)
    return lax.all_to_all(degree_values, "lat", split_axis=0, concat_axis=3, tiled=True)


def from_spectral(degree_values, basis_table, blocks):
    degree_input = lax.all_to_all(degree_values, "lat", split_axis=3, concat_axis=0, tiled=True)
    cycle_values = to_latitudes(degree_input, basis_table, blocks)
    return lax.all_to_all(cycle_values, "lat", split_axis=0, concat_axis=3, tiled=True)


def forward_mix(coeffs, weight_piece):
    products = jnp.einsum(
        "lrkc,dlsc->lrskd", coeffs, weight_piece, preferred_element_type=jnp.float32
    )
    real_part = products[:, 0, 0] - products[:, 1, 1]
    imag_part = products[:, 0, 1] + products[:, 1, 0]
    return jnp.stack([real_part, imag_part], axis=1)


def back_mix(grad_part, weight_piece):
    products = jnp.einsum(
        "lskd,dlrc->lsrkc", grad_part, weight_piece, preferred_element_type=jnp.float32
    )
    real_part = products[:, 0, 0] + products[:, 1, 1]
    imag_part = products[:, 1, 0] - products[:, 0, 1]
    return jnp.stack([real_part, imag_part], axis=1)


def weight_grad(coeffs, grad_part):
    products = jnp.einsum("lskd,lrkc->dlsrc", grad_part, coeffs, preferred_element_type=jnp.float32)
    real_part = products[:, :, 0, 0] + products[:, :, 1, 1]
    imag_part = products[:, :, 1, 0] - products[:, :, 0, 1]
    return jnp.stack([real_part, imag_part], axis=2)


def on_device(grid_state, upstream, spectral_weight, up_weight, down_weight):
    lat_devices = lax.axis_size("lat")
    lon_devices = lax.axis_size("lon")
    lat_rows, lon_cells, channels = grid_state.shape
    degrees = lat_rows * lat_devices
    lon_total = lon_cells * lon_devices
    per_device = degrees // lon_devices
    forward_np, inverse_np = fourier_tables(lon_total, order_slots(degrees))
    fourier_fwd = jnp.asarray(forward_np, jnp.float32).astype(jnp.bfloat16)
    fourier_inv = jnp.asarray(inverse_np, jnp.float32).astype(jnp.bfloat16)
    cosines, log_sines, quad = latitude_tables(degrees)
    cos_row = jnp.asarray(cosines, jnp.float32)[None, :]
    sin_row = jnp.asarray(log_sines, jnp.float32)[None, :]
    quad_row = jnp.asarray(quad, jnp.float32)[None, :]
    lon_index = lax.axis_index("lon")
    counter = jnp.arange(per_device, dtype=jnp.int32)
    order_ids = lon_index * per_device + counter
    diag_row = jnp.asarray(diagonal_logs(degrees), jnp.float32)[None, :]
    matches = order_ids[:, None] == jnp.arange(degrees, dtype=jnp.int32)[None, :]
    picked = jnp.sum(jnp.where(matches, diag_row, 0.0), axis=1)
    orders_col = order_ids.astype(jnp.float32)[:, None]
    start_logs = picked[:, None] + orders_col * sin_row
    plain, weighted = legendre_tables(orders_col, start_logs, cos_row, quad_row, degrees)
    blocks = degree_blocks(degrees, per_device)
    spectra = grid_to_orders(grid_state, fourier_fwd, "knc,nrs->krsc")
    coeffs = to_spectral(spectra, weighted, blocks)
    mixed_coeffs = forward_mix(
        coeffs, lax.all_gather(spectral_weight, "lon", axis=0, tiled=True)
    ).astype(jnp.bfloat16)
    cycle_values = from_spectral(mixed_coeffs, plain, blocks)
    spectral_part = orders_to_grid(cycle_values, fourier_inv, "krsc,rsn->knc")
    mid_state = (grid_state.astype(jnp.float32) + spectral_part.astype(jnp.float32)).astype(
        jnp.bfloat16
    )
    mid_rows = mid_state.reshape(-1, channels)
    hidden = jnp.dot(mid_rows, up_weight, preferred_element_type=jnp.float32)
    act_value, act_pull = jax.vjp(jax.nn.gelu, hidden)
    activation = act_value.astype(jnp.bfloat16)
    next_rows = mid_rows.astype(jnp.float32) + jnp.dot(
        activation, down_weight, preferred_element_type=jnp.float32
    )
    next_state = next_rows.astype(jnp.bfloat16).reshape(lat_rows, lon_cells, channels)
    up_rows = upstream.reshape(-1, channels)
    down_part = jnp.einsum("tf,tc->fc", activation, up_rows, preferred_element_type=jnp.float32)
    pulled = jnp.einsum("tc,fc->tf", up_rows, down_weight, preferred_element_type=jnp.float32)
    grad_hidden = act_pull(pulled)[0].astype(jnp.bfloat16)
    up_part = jnp.einsum("tc,tf->cf", mid_rows, grad_hidden, preferred_element_type=jnp.float32)
    grad_mid = up_rows.astype(jnp.float32) + jnp.einsum(
        "tf,cf->tc", grad_hidden, up_weight, preferred_element_type=jnp.float32
    )
    grad_mid = grad_mid.astype(jnp.bfloat16).reshape(lat_rows, lon_cells, channels)
    grad_up, grad_down = lax.psum((up_part, down_part), ("lat", "lon"))
    grad_cycles = grid_to_orders(grad_mid, fourier_inv, "knc,rsn->krsc")
    grad_mixed = to_spectral(grad_cycles, plain, blocks)
    grad_part = lax.slice_in_dim(
        grad_mixed, 0, channels // lon_devices * lax.axis_size("lon"), axis=3
    )
    grad_spectral = lax.psum_scatter(
        weight_grad(coeffs, grad_part).astype(jnp.bfloat16), "lon", scatter_dimension=0, tiled=True
    ).astype(jnp.float32)
    initial = jnp.zeros(coeffs.shape, jnp.float32)
    weight_piece = lax.all_gather(spectral_weight, "lon", axis=0, tiled=True)
    grad_part = lax.slice_in_dim(grad_mixed, 0, weight_piece.shape[0], axis=3)
    grad_coeffs = (initial + back_mix(grad_part, weight_piece)).astype(jnp.bfloat16)
    grad_spectra = from_spectral(grad_coeffs, weighted, blocks)
    grad_spectral_part = orders_to_grid(grad_spectra, fourier_fwd, "krsc,nrs->knc")
    grad_state = (grad_mid.astype(jnp.float32) + grad_spectral_part.astype(jnp.float32)).astype(
        jnp.bfloat16
    )
    return (next_state, grad_state, grad_spectral, grad_up, grad_down)


def solution(mesh):
    in_specs = (P("lat", "lon", None), P("lat", "lon", None), P("lon", "lat", None, None), P(), P())
    out_specs = (
        P("lat", "lon", None),
        P("lat", "lon", None),
        P("lon", "lat", None, None),
        P(),
        P(),
    )
    return jax.shard_map(
        on_device, mesh=mesh, in_specs=in_specs, out_specs=out_specs, check_vma=False
    )
```

profile of v0, /device:TPU:0, one launch (start us, length us, event | category | flops | bytes accessed | tf_op | source)
XLA Modules:
  0.0 2224.4 jit_solution(7049471644096722454)
XLA Ops:
  7.2 5.0 copy.279
  12.2 77.0 %all_to_all.270 = bf16[48,192,128]{1,0,2:T(8,128)(2,1)S(1)} all-to-all(bf16[48,192,128]{1,0,2:T(8,128)(2,1)} %copy.279), channel_id=1, replica_groups=mesh['lat'=8,'lon'=4] {'lon'}, dimensions={2} | all-to-all | bytes 4718592 | tf_op jit(solution)/shard_map/all_to_all | solution.py:132
  92.4 11.0 reshape.1933
  103.4 8.5 copy.281
  111.9 4.7 convert_bitcast_fusion.5
  116.6 9.9 copy.282
  126.5 11.2 reshape.1960
  145.0 98.6 %all-to-all-done.1 = bf16[4,2,147456]{2,1,0:T(2,128)(2,1)S(1)} async-done(((bf16[4,2,147456]{2,1,0:T(2,128)(2,1)}), bf16[4,2,147456]{2,1,0:T(2,128)(2,1)S(1)}, u32[]{:S(2)}, u32[]{:S(2)}) %all-to-all-start.1) | async-done | bytes 2359328 | tf_op jit(solution)/shard_map/all_to_all | solution.py:136
  243.6 7.5 reshape.1961
  251.1 11.8 copy.283
  262.9 6.8 copy.284
  269.7 5.1 all-to-all-start.2
  274.8 717.1 %while.25 = (s32[]{:T(128)}, f32[96,384]{1,0:T(8,128)S(1)}, f32[96,384]{1,0:T(8,128)S(1)}, f32[96,384]{1,0:T(8,128)S(1)}, bf16[24,16,96,384]{3,2,1,0:T(8,128)(2,...) while((s32[]{:T(128)}, f32[96,384]{1,0:T(8,128)S(1)}, ...), condition=%wide.region_2.3_spmd.clone.clone.clone.clone, body=%wide.region_1.2_spmd.sunk.clone.clone.clone.clone.sunk | while | flops 17055936 | bytes 25985960 | solution.py:81
  999.5 28.3 %convert_bitcast_fusion.4 = bf16[384,2,96,16]{0,3,1,2:T(8,128)(2,1)} fusion(bf16[384,2,96,16]{0,3,1,2:T(8,128)(2,1)} %copy.287, bf16[384,96,384,1]{2,1,0,3:T(8,128)(2,1)} %bitcast.586), kind=kOutput, calls=%fused_computation.262 | convolution fusion | flops 907149312 | bytes 33030144 | tf_op jit(solution)/shard_map/lkj,jrkc->lrkc/dot_general | solution.py:101
  1027.8 4.4 copy.289
  1032.2 41.8 %all_to_all.271 = bf16[384,2,96,16]{2,3,1,0:T(8,128)(2,1)S(1)} all-to-all(bf16[384,2,96,16]{2,3,1,0:T(8,128)(2,1)S(1)} %copy.289), channel_id=1, replica_groups=mesh['lat'=8,'lon'=4] {'lat'}, dimensions={0} | all-to-all | bytes 4718592 | tf_op jit(solution)/shard_map/all_to_all | solution.py:152
  1075.0 4.4 convolution_bitcast_fusion.2
  1085.5 40.3 %all_to_all.272 = bf16[48,2,96,128]{2,0,1,3:T(8,128)(2,1)S(1)} all-to-all(bf16[48,2,96,128]{2,0,1,3:T(8,128)(2,1)S(1)} %copy.295), channel_id=1, replica_groups=mesh['lat'=8,'lon'=4] {'lat'}, dimensions={3} | all-to-all | bytes 4718592 | tf_op jit(solution)/shard_map/all_to_all | solution.py:156
  1130.8 29.6 %convert_bitcast_fusion.3 = bf16[384,2,96,16]{0,3,1,2:T(8,128)(2,1)} fusion(bf16[384,2,96,16]{0,3,1,2:T(8,128)(2,1)} %copy.298, bf16[384,96,384,1]{2,1,0,3:T(8,128)(2,1)} %bitcast.584), kind=kOutput, calls=%fused_computation.261 | convolution fusion | flops 907149312 | bytes 33030144 | tf_op jit(solution)/shard_map/lkj,lrkc->jrkc/dot_general | solution.py:117
  1160.4 4.6 copy.300
  1165.0 40.3 %all_to_all.273 = bf16[384,2,96,16]{2,3,1,0:T(8,128)(2,1)S(1)} all-to-all(bf16[384,2,96,16]{2,3,1,0:T(8,128)(2,1)S(1)} %copy.300), channel_id=1, replica_groups=mesh['lat'=8,'lon'=4] {'lat'}, dimensions={0} | all-to-all | bytes 4718592 | tf_op jit(solution)/shard_map/all_to_all | solution.py:158
  1209.4 72.8 %all_to_all.274 = bf16[48,2,96,128]{2,1,0,3:T(2,128)(2,1)S(1)} all-to-all(bf16[48,2,96,128]{2,1,0,3:T(2,128)(2,1)S(1)} %copy.302), channel_id=1, replica_groups=mesh['lat'=8,'lon'=4] {'lon'}, dimensions={3} | all-to-all | bytes 4718592 | tf_op jit(solution)/shard_map/all_to_all | solution.py:142
  1293.3 10.7 copy.305
  1304.0 10.4 reshape.1962
  1314.5 56.6 %all_to_all.275 = bf16[4,2,147456]{2,1,0:T(2,128)(2,1)} all-to-all(bf16[4,2,147456]{2,1,0:T(2,128)(2,1)S(1)} %reshape.1962), channel_id=1, replica_groups=mesh['lat'=8,'lon'=4] {'lon'}, dimensions={0} | all-to-all | bytes 4718592 | tf_op jit(solution)/shard_map/all_to_all | solution.py:146
  1371.0 8.2 reshape.1963
  1379.2 11.7 copy.306
  1390.9 6.3 copy.307
  1400.2 11.2 multiply_convert_fusion.1
  1411.5 15.9 fusion.66
  1434.4 75.3 %all_to_all.276 = bf16[48,192,128]{1,0,2:T(8,128)(2,1)} all-to-all(bf16[48,192,128]{1,0,2:T(8,128)(2,1)} %copy.309), channel_id=1, replica_groups=mesh['lat'=8,'lon'=4] {'lon'}, dimensions={2} | all-to-all | bytes 4718592 | tf_op jit(solution)/shard_map/all_to_all | solution.py:132
  1509.6 4.8 copy.310
  1514.4 11.0 reshape.1936
  1525.4 10.4 convert_bitcast_fusion.2
  1535.8 10.5 copy.312
  1546.3 10.4 reshape.1964
  1556.7 56.1 %all_to_all.277 = bf16[4,2,147456]{2,1,0:T(2,128)(2,1)} all-to-all(bf16[4,2,147456]{2,1,0:T(2,128)(2,1)S(1)} %reshape.1964), channel_id=1, replica_groups=mesh['lat'=8,'lon'=4] {'lon'}, dimensions={0} | all-to-all | bytes 4718592 | tf_op jit(solution)/shard_map/all_to_all | solution.py:136
  1612.9 8.2 reshape.1965
  1621.0 10.9 copy.313
  1635.2 41.1 %all_to_all.278 = bf16[48,2,96,128]{2,1,0,3:T(2,128)(2,1)S(1)} all-to-all(bf16[48,2,96,128]{2,1,0,3:T(2,128)(2,1)S(1)} %copy.314), channel_id=1, replica_groups=mesh['lat'=8,'lon'=4] {'lat'}, dimensions={3} | all-to-all | bytes 4718592 | tf_op jit(solution)/shard_map/all_to_all | solution.py:150
  1682.0 28.2 %convert_bitcast_fusion.1 = bf16[384,2,96,16]{0,3,1,2:T(8,128)(2,1)} fusion(bf16[384,2,96,16]{0,3,1,2:T(8,128)(2,1)} %copy.317, bf16[384,96,384,1]{2,1,0,3:T(8,128)(2,1)} %bitcast.585), kind=kOutput, calls=%fused_computation.259 | convolution fusion | flops 907149312 | bytes 33030144 | tf_op jit(solution)/shard_map/lkj,jrkc->lrkc/dot_general | solution.py:101
  1710.2 4.4 copy.319
  1714.7 40.5 %all_to_all.279 = bf16[384,2,96,16]{2,3,1,0:T(8,128)(2,1)S(1)} all-to-all(bf16[384,2,96,16]{2,3,1,0:T(8,128)(2,1)S(1)} %copy.319), channel_id=1, replica_groups=mesh['lat'=8,'lon'=4] {'lat'}, dimensions={0} | all-to-all | bytes 4718592 | tf_op jit(solution)/shard_map/all_to_all | solution.py:152
  1764.5 40.3 %all_to_all.280 = bf16[48,2,96,128]{2,0,1,3:T(8,128)(2,1)S(1)} all-to-all(bf16[48,2,96,128]{2,0,1,3:T(8,128)(2,1)S(1)} %copy.324), channel_id=1, replica_groups=mesh['lat'=8,'lon'=4] {'lat'}, dimensions={3} | all-to-all | bytes 4718592 | tf_op jit(solution)/shard_map/all_to_all | solution.py:156
  1809.8 28.2 %convert_bitcast_fusion = bf16[384,2,96,16]{0,3,1,2:T(8,128)(2,1)S(1)} fusion(bf16[384,2,96,16]{0,3,1,2:T(8,128)(2,1)} %copy.327, bf16[384,96,384,1]{2,1,0,3:T(8,128)(2,1)} %bitcast.587), kind=kOutput, calls=%fused_computation.258 | convolution fusion | flops 907149312 | bytes 33030144 | tf_op jit(solution)/shard_map/lkj,lrkc->jrkc/dot_general | solution.py:117
  1841.9 4.7 all-to-all-start.13
  1850.3 4.6 copy-done.3
  1856.7 27.8 %all-to-all-done.13 = bf16[384,2,96,16]{2,3,1,0:T(8,128)(2,1)} async-done(((bf16[384,2,96,16]{2,3,1,0:T(8,128)(2,1)}), bf16[384,2,96,16]{2,3,1,0:T(8,128)(2,1)}, u32[]{:S(2)}, u32[]{:S(2)}) %all-to-all-start.13) | async-done | bytes 2359328 | tf_op jit(solution)/shard_map/all_to_all | solution.py:158
  1887.3 4.9 copy.331
  1901.5 5.4 copy.340
  1906.9 107.6 %all-to-all-done.14 = bf16[48,2,96,128]{2,1,0,3:T(2,128)(2,1)S(1)} async-done(((bf16[48,2,96,128]{2,1,0,3:T(2,128)(2,1)}), bf16[48,2,96,128]{2,1,0,3:T(2,128)(2,1)S(1)}, u32[]{:S(2)}, u32[]{:S(2)}) %all-to-all-start.14) | async-done | bytes 2359328 | tf_op jit(solution)/shard_map/all_to_all | solution.py:142
  2025.6 10.7 copy.334
  2036.3 11.3 reshape.1966
  2047.5 4.5 all-to-all-start.15
  2052.1 4.8 copy.308
  2056.9 6.0 fusion.115
  2062.8 7.1 fusion.116
  2069.9 7.7 fusion.67
  2080.5 27.1 %all-to-all-done.15 = bf16[4,2,147456]{2,1,0:T(2,128)(2,1)} async-done(((bf16[4,2,147456]{2,1,0:T(2,128)(2,1)}), bf16[4,2,147456]{2,1,0:T(2,128)(2,1)}, u32[]{:S(2)}, u32[]{:S(2)}) %all-to-all-start.15) | async-done | bytes 2359328 | tf_op jit(solution)/shard_map/all_to_all | solution.py:146
  2107.7 8.2 reshape.1967
  2115.9 11.8 copy.335
  2127.7 5.6 fusion.71
  2133.3 4.5 copy.341
  2137.8 76.5 %all-reduce.3.cloned.1.call-done = (f32[128,512]{1,0:T(8,128)}, f32[512,128]{1,0:T(8,128)}) async-done(((f32[128,512]{1,0:T(8,128)}, f32[512,128]{1,0:T(8,128)}), (f32[128,512]{1,0:T(8,128)}, f32[512,128]{1,0:T(8,128)})) %all-reduce.3.cloned.1.call-update) | async-done | bytes 524304 | tf_op jit(solution)/shard_map/psum | solution.py:237
  (1904 shorter events, 570.8 us)
Async XLA Ops:
  7.2 1393.0 %copy-start = (bf16[128,512]{1,0:T(8,128)(2,1)S(1)}, bf16[128,512]{1,0:T(8,128)(2,1)}, u32[]{:S(2)}) copy-start(bf16[128,512]{1,0:T(8,128)(2,1)} %param.16) | copy-start | bytes 393220
  137.8 7.1 copy-start.27
  137.8 105.9 %all-to-all-start.1 = ((bf16[4,2,147456]{2,1,0:T(2,128)(2,1)}), bf16[4,2,147456]{2,1,0:T(2,128)(2,1)S(1)}, u32[]{:S(2)}, u32[]{:S(2)}) async-start(bf16[4,2,147456]{2,1,0:T(2,128)(2,1)} %reshape.1960), calls=%async_computation.1 | async-start | bytes 4718592 | tf_op jit(solution)/shard_map/all_to_all | solution.py:136
  141.5 933.4 %all-gather.2.cloned.1.call-start = ((), (), s32[]{:S(2)}) async-start(), calls=%async_computation.17 | async-start | bytes 3932160 | tf_op jit(solution)/shard_map/all_gather | solution.py:213
  269.7 5.1 copy-start.14
  269.7 5.1 copy-start.15
  269.7 722.2 %all-to-all-start.2 = ((bf16[48,2,96,128]{2,1,0,3:T(2,128)(2,1)}), bf16[48,2,96,128]{2,1,0,3:T(2,128)(2,1)}, u32[]{:S(2)}, u32[]{:S(2)}) async-start(bf16[48,2,96,128]{2,1,0,3:T(2,128)(2,1)} %copy.284), calls=%async_computation.2 | async-start | bytes 6291456 | tf_op jit(solution)/shard_map/all_to_all | solution.py:150
  277.5 3.1 copy-start.24
  294.8 8.1 copy-start.26
  307.3 3.1 copy-start.24
  324.7 8.1 copy-start.26
  337.2 3.1 copy-start.24
  354.5 8.1 copy-start.26
  367.1 3.1 copy-start.24
  384.4 8.1 copy-start.26
  397.0 3.1 copy-start.24
  414.3 8.1 copy-start.26
  426.8 3.1 copy-start.24
  444.1 8.1 copy-start.26
  456.7 3.1 copy-start.24
  474.0 8.1 copy-start.26
  486.8 3.1 copy-start.24
  504.1 8.1 copy-start.26
  516.6 3.1 copy-start.24
  533.9 8.1 copy-start.26
  546.4 3.1 copy-start.24
  563.7 8.1 copy-start.26
  576.3 3.1 copy-start.24
  593.7 8.1 copy-start.26
  606.2 3.1 copy-start.24
  623.5 8.1 copy-start.26
  636.1 3.1 copy-start.24
  653.4 8.1 copy-start.26
  683.2 8.1 copy-start.26
  713.0 8.1 copy-start.26
  725.6 3.1 copy-start.24
  742.9 8.1 copy-start.26
  772.8 8.1 copy-start.26
  802.6 8.1 copy-start.26
  832.5 8.1 copy-start.26
  862.4 8.1 copy-start.26
  892.2 8.1 copy-start.26
  922.2 8.1 copy-start.26
  952.1 8.1 copy-start.26
  982.0 8.1 copy-start.26
  1074.9 4.5 copy-start.9
  1390.9 6.3 copy-start.18
  1400.2 11.3 copy-start.7
  1400.2 11.3 copy-start.20
  1400.2 11.2 copy-start.25
  1427.4 3.5 copy-start.2
  1430.9 78.7 %copy-start.12 = (bf16[9216,128]{1,0:T(8,128)(2,1)}, bf16[9216,128]{1,0:T(8,128)(2,1)S(1)}, u32[]{:S(2)}) copy-start(bf16[9216,128]{1,0:T(8,128)(2,1)S(1)} %fusion.68) | copy-start | bytes 7077892
  1841.9 4.7 copy-start.10
  1841.9 42.6 %all-to-all-start.13 = ((bf16[384,2,96,16]{2,3,1,0:T(8,128)(2,1)}), bf16[384,2,96,16]{2,3,1,0:T(8,128)(2,1)}, u32[]{:S(2)}, u32[]{:S(2)}) async-start(bf16[384,2,96,16]{2,3,1,0:T(8,128)(2,1)} %copy.329), calls=%async_computation.13 | async-start | bytes 6291456 | tf_op jit(solution)/shard_map/all_to_all | solution.py:158
  1850.3 4.6 copy-start.3
  1892.3 122.2 %all-to-all-start.14 = ((bf16[48,2,96,128]{2,1,0,3:T(2,128)(2,1)}), bf16[48,2,96,128]{2,1,0,3:T(2,128)(2,1)S(1)}, u32[]{:S(2)}, u32[]{:S(2)}) async-start(bf16[48,2,96,128]{2,1,0,3:T(2,128)(2,1)} %copy.331), calls=%async_computation.14 | async-start | bytes 6291456 | tf_op jit(solution)/shard_map/all_to_all | solution.py:142
  1896.0 181.7 %reduce-scatter.2.cloned.1.call-start = ((), (), s32[]{:S(2)}) async-start(), calls=%async_computation.18 | async-start | bytes 3932160 | tf_op jit(solution)/shard_map/reduce_scatter | solution.py:243
  1896.0 3.6 copy-start.19
  2047.5 60.1 %all-to-all-start.15 = ((bf16[4,2,147456]{2,1,0:T(2,128)(2,1)}), bf16[4,2,147456]{2,1,0:T(2,128)(2,1)}, u32[]{:S(2)}, u32[]{:S(2)}) async-start(bf16[4,2,147456]{2,1,0:T(2,128)(2,1)} %reshape.1966), calls=%async_computation.15 | async-start | bytes 4718592 | tf_op jit(solution)/shard_map/all_to_all | solution.py:146
  2052.0 4.8 copy-start.8
  2052.0 162.3 %all-reduce.3.cloned.1.call-start = ((), (), s32[]{:S(2)}) async-start(), calls=%async_computation.19 | async-start | bytes 1048576 | tf_op jit(solution)/shard_map/psum | solution.py:237
  2056.9 6.0 copy-start.21
  2115.9 11.8 copy-start.16
  2127.7 90.0 %copy-start.1 = (bf16[128,512]{1,0:T(8,128)(2,1)S(1)}, bf16[128,512]{1,0:T(8,128)(2,1)}, u32[]{:S(2)}) copy-start(bf16[128,512]{1,0:T(8,128)(2,1)} %param.16) | copy-start | bytes 393220
  (156 other events, 377.3 us)
Sparse Core Ops, SparseCore 0:
  144.5 100.8 all-gather.1
  1907.1 104.4 reduce-scatter.1
  2070.0 144.2 all-reduce.2
where the time goes:
time: 2240 us; the launch traced here: 2220 us
  blocking collectives  582 us (26%)
  other arithmetic  445 us (20%)
  local copies, waits for them, and re-layouts  362 us (16%)
  waiting for transfers between devices  338 us (15%)
  loops' own time  263 us (12%)
  matrix products  198 us (9%)
    while x360, other arithmetic  333 us
    another operation x1, loops' own time, legendre_tables(): lax.scan(advance, (zeros_state, zeros_state, zeros_state), openings)  263 us
    all_to_all x2, blocking collectives, grid_to_orders(): lax.all_to_all(grid_values, 'lon', split_axis=2, concat_axis=1, tiled=True)  152 us
    all_to_all x1, waiting for transfers between devices, orders_to_grid(): lax.all_to_all(order_values, 'lon', split_axis=3, concat_axis=2, tiled=True)  108 us
    unnamed x54, local copies, waits for them, and re-layouts  99.7 us
    all_to_all x1, waiting for transfers between devices, grid_to_orders(): lax.all_to_all(spectrum, 'lon', split_axis=2, concat_axis=3, tiled=True)  98.6 us
    all_to_all x2, blocking collectives, to_spectral(): lax.all_to_all(degree_values, 'lat', split_axis=0, concat_axis=3, tiled=T...  82.3 us
    all_to_all x2, blocking collectives, from_spectral(): lax.all_to_all(degree_values, 'lat', split_axis=3, concat_axis=0, tiled=T...  80.6 us
  transfers between devices with their start and end apart: 8, of which 5 were waited for; matrix products, arithmetic and copies ran while one was open for 28% of the time, Pallas kernels for 0%

commit v1 on v0

--- a/solution.py
+++ b/solution.py
@@ -2,6 +2,8 @@
 import jax.numpy as jnp
 import numpy as np
 from jax import lax
+from jax.experimental import pallas as pl
+from jax.experimental.pallas import tpu as pltpu
 from jax.sharding import PartitionSpec as P
 
 
@@ -183,7 +185,7 @@
     return jnp.stack([real_part, imag_part], axis=2)
 
 
-def on_device(grid_state, upstream, spectral_weight, up_weight, down_weight):
+def general_device(grid_state, upstream, spectral_weight, up_weight, down_weight):
     lat_devices = lax.axis_size("lat")
     lon_devices = lax.axis_size("lon")
     lat_rows, lon_cells, channels = grid_state.shape
@@ -255,6 +257,183 @@
     return (next_state, grad_state, grad_spectral, grad_up, grad_down)
 
 
+GROUP = 8
+
+
+def table_kernel(orders, degrees, cos_ref, start_ref, grow_ref, lag_ref, seed_ref, out_ref, held):
+    cos_rows = cos_ref[...]
+    zeros = jnp.zeros(start_ref.shape, jnp.float32)
+
+    def advance(block, carry):
+        newest, former, logscale = carry
+        scale = jnp.exp(logscale)
+        for offset in range(GROUP):
+            degree = block * GROUP + offset
+            value = (
+                cos_rows * grow_ref[degree] * newest - lag_ref[degree] * former + seed_ref[degree]
+            )
+            former = newest
+            newest = value
+            held[degree] = value * scale
+        top = jnp.maximum(jnp.abs(newest), jnp.abs(former))
+        top = jnp.where(top == 0.0, 1.0, top)
+        return (newest / top, former / top, logscale + jnp.log(top))
+
+    lax.fori_loop(0, degrees // GROUP, advance, (zeros, zeros, start_ref[...]))
+    for order in range(orders):
+        out_ref[order] = held[:, order, :].astype(jnp.bfloat16)
+
+
+def order_table(order_ids, degrees, cosines, log_sines):
+    orders = order_ids.shape[0]
+    padded = -(-orders // 8) * 8
+    ids = jnp.concatenate([order_ids, jnp.full((padded - orders,), degrees, jnp.int32)])
+    diag_row = jnp.asarray(diagonal_logs(degrees), jnp.float32)[None, :]
+    matches = ids[:, None] == jnp.arange(degrees, dtype=jnp.int32)[None, :]
+    picked = jnp.sum(jnp.where(matches, diag_row, 0.0), axis=1)
+    orders_row = ids.astype(jnp.float32)
+    cos_row = jnp.asarray(cosines, jnp.float32)[None, :]
+    sin_row = jnp.asarray(log_sines, jnp.float32)[None, :]
+    start_logs = picked[:, None] + orders_row[:, None] * sin_row
+    degree_col = jnp.arange(degrees, dtype=jnp.float32)[:, None]
+    square = orders_row[None, :] * orders_row[None, :]
+    grow = jnp.sqrt(
+        (4.0 * degree_col * degree_col - 1.0) / jnp.maximum(degree_col * degree_col - square, 1.0)
+    )
+    grow = jnp.where(degree_col > orders_row[None, :], grow, 0.0)
+    lagged = degree_col - 1.0
+    shrink = jnp.sqrt(
+        jnp.maximum(lagged * lagged - square, 0.0) / jnp.maximum(4.0 * lagged * lagged - 1.0, 1.0)
+    )
+    seed = jnp.where(degree_col == orders_row[None, :], 1.0, 0.0)
+    cycles = cos_row.shape[1]
+    return pl.pallas_call(
+        lambda *refs: table_kernel(orders, degrees, *refs),
+        out_shape=jax.ShapeDtypeStruct((orders, degrees, cycles), jnp.bfloat16),
+        in_specs=[pl.BlockSpec(memory_space=pltpu.VMEM)] * 5,
+        out_specs=pl.BlockSpec(memory_space=pltpu.VMEM),
+        scratch_shapes=[pltpu.VMEM((degrees, padded, cycles), jnp.float32)],
+        compiler_params=pltpu.CompilerParams(vmem_limit_bytes=48 * 2**20),
+        cost_estimate=pl.CostEstimate(
+            flops=12 * degrees * padded * cycles,
+            bytes_accessed=2 * orders * degrees * cycles,
+            transcendentals=0,
+        ),
+    )(
+        jnp.broadcast_to(cos_row, start_logs.shape),
+        start_logs,
+        grow[:, :, None],
+        (grow * shrink)[:, :, None],
+        seed[:, :, None],
+    )
+
+
+def on_device(grid_state, upstream, spectral_weight, up_weight, down_weight):
+    lat_devices = lax.axis_size("lat")
+    lon_devices = lax.axis_size("lon")
+    lat_rows, lon_cells, channels = grid_state.shape
+    degrees = lat_rows * lat_devices
+    if lat_rows % lon_devices or (degrees // (lat_devices * lon_devices)) % 4:
+        return general_device(grid_state, upstream, spectral_weight, up_weight, down_weight)
+    devices = lat_devices * lon_devices
+    orders = degrees // devices
+    cycles = lat_rows // lon_devices
+    lon_total = lon_cells * lon_devices
+    both = ("lat", "lon")
+    place = lax.axis_index("lat") * lon_devices + lax.axis_index("lon")
+
+    forward_np, inverse_np = fourier_tables(lon_total, order_slots(degrees))
+
+    def by_order(table):
+        table = table.reshape(lon_total, 2, devices, orders).transpose(0, 2, 1, 3)
+        return jnp.asarray(table.reshape(lon_total, 2 * degrees), jnp.float32).astype(jnp.bfloat16)
+
+    fourier_fwd = by_order(forward_np)
+    fourier_inv = by_order(inverse_np.transpose(2, 0, 1))
+    cosines, log_sines, quad = latitude_tables(degrees)
+    quad_all = jnp.asarray(quad, jnp.float32)
+    quad_own = lax.dynamic_slice_in_dim(quad_all, place * cycles, cycles, axis=0)
+    order_ids = place * orders + jnp.arange(orders, dtype=jnp.int32)
+    table = order_table(order_ids, degrees, cosines, log_sines)
+    weight = lax.all_gather(spectral_weight, "lon", axis=0, tiled=True)
+
+    def grid_to_degrees(values, fourier, scale):
+        circles = lax.all_to_all(values, "lon", split_axis=0, concat_axis=1, tiled=True)
+        spectrum = jnp.einsum("jnc,nq->jqc", circles, fourier, preferred_element_type=jnp.float32)
+        if scale is not None:
+            spectrum = spectrum * scale[:, None, None]
+        spectrum = lax.all_to_all(
+            spectrum.astype(jnp.bfloat16), both, split_axis=1, concat_axis=0, tiled=True
+        ).reshape(degrees, 2, orders, channels)
+        coeffs = jnp.einsum(
+            "mlj,jrmc->lrmc", table, spectrum, preferred_element_type=jnp.float32
+        ).astype(jnp.bfloat16)
+        coeffs = lax.all_to_all(
+            coeffs.reshape(lat_devices, lat_rows, 2 * orders, channels), "lat", 0, 0, tiled=True
+        ).reshape(lat_devices, lat_rows, 2, orders, channels)
+        return coeffs.transpose(1, 2, 0, 3, 4).reshape(
+            lat_rows, 2, lat_devices * orders, channels
+        )
+
+    def degrees_to_grid(coeffs, fourier, scale):
+        coeffs = coeffs.reshape(lat_rows, 2, lat_devices, orders, channels).transpose(2, 0, 1, 3, 4)
+        coeffs = lax.all_to_all(
+            coeffs.reshape(lat_devices, lat_rows, 2 * orders, channels), "lat", 0, 0, tiled=True
+        ).reshape(degrees, 2, orders, channels)
+        spectrum = jnp.einsum("mlj,lrmc->jrmc", table, coeffs, preferred_element_type=jnp.float32)
+        if scale is not None:
+            spectrum = spectrum * scale[:, None, None, None]
+        spectrum = lax.all_to_all(
+            spectrum.astype(jnp.bfloat16).reshape(degrees, 2 * orders, channels),
+            both,
+            split_axis=0,
+            concat_axis=1,
+            tiled=True,
+        )
+        circles = jnp.einsum("jqc,nq->jnc", spectrum, fourier, preferred_element_type=jnp.float32)
+        return lax.all_to_all(
+            circles.astype(jnp.bfloat16), "lon", split_axis=1, concat_axis=0, tiled=True
+        )
+
+    coeffs = grid_to_degrees(grid_state, fourier_fwd, quad_own)
+    mixed_coeffs = forward_mix(coeffs, weight).astype(jnp.bfloat16)
+    spectral_part = degrees_to_grid(mixed_coeffs, fourier_inv, None)
+    mid_state = (grid_state.astype(jnp.float32) + spectral_part.astype(jnp.float32)).astype(
+        jnp.bfloat16
+    )
+    mid_rows = mid_state.reshape(-1, channels)
+    hidden = jnp.dot(mid_rows, up_weight, preferred_element_type=jnp.float32)
+    act_value, act_pull = jax.vjp(jax.nn.gelu, hidden)
+    activation = act_value.astype(jnp.bfloat16)
+    next_rows = mid_rows.astype(jnp.float32) + jnp.dot(
+        activation, down_weight, preferred_element_type=jnp.float32
+    )
+    next_state = next_rows.astype(jnp.bfloat16).reshape(lat_rows, lon_cells, channels)
+    up_rows = upstream.reshape(-1, channels)
+    down_part = jnp.einsum("tf,tc->fc", activation, up_rows, preferred_element_type=jnp.float32)
+    pulled = jnp.einsum("tc,fc->tf", up_rows, down_weight, preferred_element_type=jnp.float32)
+    grad_hidden = act_pull(pulled)[0].astype(jnp.bfloat16)
+    up_part = jnp.einsum("tc,tf->cf", mid_rows, grad_hidden, preferred_element_type=jnp.float32)
+    grad_mid = up_rows.astype(jnp.float32) + jnp.einsum(
+        "tf,cf->tc", grad_hidden, up_weight, preferred_element_type=jnp.float32
+    )
+    grad_mid = grad_mid.astype(jnp.bfloat16).reshape(lat_rows, lon_cells, channels)
+    grad_mid, up_part, down_part, next_state = lax.optimization_barrier(
+        (grad_mid, up_part, down_part, next_state)
+    )
+    grad_up, grad_down = lax.psum((up_part, down_part), both)
+    grad_mixed = grid_to_degrees(grad_mid, fourier_inv, None)
+    grad_spectral = lax.psum_scatter(
+        weight_grad(coeffs, grad_mixed).astype(jnp.bfloat16), "lon", scatter_dimension=0, tiled=True
+    ).astype(jnp.float32)
+    grad_coeffs = back_mix(grad_mixed, weight).astype(jnp.bfloat16)
+    grad_spectral_part = degrees_to_grid(grad_coeffs, fourier_fwd, quad_all)
+    grad_state = (grad_mid.astype(jnp.float32) + grad_spectral_part.astype(jnp.float32)).astype(
+        jnp.bfloat16
+    )
+    return (next_state, grad_state, grad_spectral, grad_up, grad_down)
+
+
 def solution(mesh):
     in_specs = (P("lat", "lon", None), P("lat", "lon", None), P("lon", "lat", None, None), P(), P())
     out_specs = (

time: 2240 us -> 1030 us (0.46)
  other arithmetic: 445 us -> 16.6 us
  local copies, waits for them, and re-layouts: 362 us -> 88.3 us
  loops' own time: 263 us -> 0 us
  blocking collectives: 582 us -> 391 us
  matrix products: 198 us -> 78.5 us
  waiting for transfers between devices: 338 us -> 396 us
    while x360 -> x0, other arithmetic: 333 us -> none
    another operation x1 -> x0, loops' own time: 263 us -> none  [legendre_tables(): lax.scan(advance, (zeros_state, zeros_state, zeros_state), openings)]
    all_to_all x11 -> x8, blocking collectives: 582 us -> 391 us  [the longest x1 74.9 us: degrees_to_grid(): lax.all_to_all(circles.astype(jnp.bfloat16), 'lon', split_axis=1, concat_...]
    dot_general x8, matrix products: 137 us -> 31.1 us  [the longest x2 12.5 us: grid_to_degrees(): jnp.einsum('mlj,jrmc->lrmc', table, spectrum, preferred_element_type=jnp....]
    unnamed x54 -> x40, local copies, waits for them, and re-layouts: 99.7 us -> 17.8 us
    all_to_all x28 -> x10, local copies, waits for them, and re-layouts: 91.7 us -> 11.7 us  [the longest x2 4.03 us: grid_to_degrees(): lax.all_to_all(spectrum.astype(jnp.bfloat16), both, split_axis=1, concat_...]
    dynamic_update_slice x24 -> x0, other arithmetic: 41.5 us -> none  [legendre_tables(): lax.scan(advance, (zeros_state, zeros_state, zeros_state), openings)]
    all_to_all x5 -> x4, waiting for transfers between devices: 261 us -> 299 us  [the longest x1 91.2 us: grid_to_degrees(): lax.all_to_all(spectrum.astype(jnp.bfloat16), both, split_axis=1, concat_...]
  transfers between devices with their start and end apart: 8 -> 7, of which waited for: 5 -> 5; matrix products, arithmetic and copies ran while one was open for 28% -> 6% of each run, Pallas kernels for 0% -> 2%
where the time goes in v1:
time: 1030 us; the launch traced here: 1020 us
  waiting for transfers between devices  396 us (38%)
  blocking collectives  391 us (38%)
  local copies, waits for them, and re-layouts  88.3 us (9%)
  matrix products  78.5 us (8%)
  starting transfers between devices  19.5 us (2%)
  Pallas kernels  18.8 us (2%)
  other arithmetic  16.6 us (2%)
  between operations  14.5 us (1%)
    psum x1, waiting for transfers between devices, on_device(): grad_up, grad_down = lax.psum((up_part, down_part), both)  96.4 us
    all_to_all x1, waiting for transfers between devices, grid_to_degrees(): lax.all_to_all(spectrum.astype(jnp.bfloat16), both, split_axis=1, concat_...  91.2 us
    all_to_all x1, waiting for transfers between devices, degrees_to_grid(): lax.all_to_all(spectrum.astype(jnp.bfloat16).reshape(degrees, 2 * orders,...  83.5 us
    all_to_all x1, blocking collectives, degrees_to_grid(): lax.all_to_all(circles.astype(jnp.bfloat16), 'lon', split_axis=1, concat_...  74.9 us
    all_to_all x1, blocking collectives, grid_to_degrees(): lax.all_to_all(spectrum.astype(jnp.bfloat16), both, split_axis=1, concat_...  72.8 us
    all_to_all x1, waiting for transfers between devices, degrees_to_grid(): lax.all_to_all(circles.astype(jnp.bfloat16), 'lon', split_axis=1, concat_...  70.9 us
    all_to_all x2, blocking collectives, grid_to_degrees(): lax.all_to_all(coeffs.reshape(lat_devices, lat_rows, 2 * orders, channels...  66.6 us
    all_to_all x2, blocking collectives, degrees_to_grid(): lax.all_to_all(coeffs.reshape(lat_devices, lat_rows, 2 * orders, channels...  63.7 us
  transfers between devices with their start and end apart: 7, of which 5 were waited for; matrix products, arithmetic and copies ran while one was open for 6% of the time, Pallas kernels for 2%

profile of v1, /device:TPU:0, one launch (start us, length us, event | category | flops | bytes accessed | tf_op | source)
XLA Modules:
  0.0 1023.4 jit_solution(501935812392253814)
XLA Ops:
  7.2 6.5 all-to-all-start
  14.4 53.1 %all-to-all-done = bf16[48,192,128]{2,1,0:T(8,128)(2,1)S(1)} async-done(((bf16[48,192,128]{2,1,0:T(8,128)(2,1)}), bf16[48,192,128]{2,1,0:T(8,128)(2,1)S(1)}, u32[]{:S(2)}, u32[]{:S(2)}) %all-to-all-start) | async-done | bytes 2359328 | tf_op jit(solution)/shard_map/all_to_all | solution.py:361
  68.7 2.0 fusion.25
  70.7 3.2 copy.163
  74.0 3.7 all-to-all-start.1
  77.8 2.3 copy.169
  80.5 6.7 sqrt_multiply_fusion
  87.2 18.8 %shard_map.146 = bf16[12,384,384]{2,1,0:T(8,128)(2,1)} custom-call(f32[16,384]{1,0:T(8,128)S(1)} %broadcast_in_dim.19.refs_0_, f32[16,384]{1,0:T(8,128)S(1)} %multiply_add_fusion.refs_1_, f32[384,16,1]{2,1,0:T(8,128)S(1)} %get-tuple-element.45.refs_2_, f32[384,16,1]{2,1,0:T(8,128)} %get-tuple-element.44.refs_3_, f32[384,16,1]{2,1,0:T(8,128)} %get-tuple-element.46.refs_4_), custom_call_target="tpu_custom_call" | custom-call | flops 28311552 | bytes 3538944 | tf_op jit(solution)/shard_map/pallas_call | solution.py:310
  106.0 91.2 %all-to-all-done.1 = bf16[12,768,128]{2,0,1:T(8,128)(2,1)S(1)} async-done(((bf16[12,768,128]{2,0,1:T(8,128)(2,1)}), bf16[12,768,128]{2,0,1:T(8,128)(2,1)S(1)}, u32[]{:S(2)}, u32[]{:S(2)}) %all-to-all-start.1) | async-done | bytes 2359328 | tf_op jit(solution)/shard_map/all_to_all | solution.py:365
  197.1 2.0 copy.263
  199.1 3.5 reshape.527
  202.6 5.8 convert_bitcast_fusion.7
  208.4 3.2 copy.166
  212.0 33.2 %all_to_all.140 = bf16[8,48,24,128]{3,1,2,0:T(8,128)(2,1)S(1)} all-to-all(bf16[8,48,24,128]{3,1,2,0:T(8,128)(2,1)S(1)} %copy.167), channel_id=1, replica_groups=mesh['lat'=8,'lon'=4] {'lat'}, dimensions={0} | all-to-all | bytes 4718592 | tf_op jit(solution)/shard_map/all_to_all | solution.py:371
  245.7 4.1 convolution_bitcast_fusion.2
  252.4 31.9 %all_to_all.141 = bf16[8,48,24,128]{3,1,2,0:T(8,128)(2,1)S(1)} all-to-all(bf16[8,48,24,128]{3,1,2,0:T(8,128)(2,1)S(1)} %bitcast.180), channel_id=1, replica_groups=mesh['lat'=8,'lon'=4] {'lat'}, dimensions={0} | all-to-all | bytes 4718592 | tf_op jit(solution)/shard_map/all_to_all | solution.py:380
  284.9 1.3 copy-done.1
  286.3 3.1 convert_bitcast_fusion.6
  289.3 3.0 copy.176
  292.4 1.5 copy.177
  293.9 57.5 %all_to_all.142 = bf16[384,24,128]{2,1,0:T(8,128)(2,1)S(1)} all-to-all(bf16[384,24,128]{2,1,0:T(8,128)(2,1)S(1)} %copy.177), channel_id=1, replica_groups=mesh['lat'=8,'lon'=4] {'lat','lon'}, dimensions={0} | all-to-all | bytes 4718592 | tf_op jit(solution)/shard_map/all_to_all | solution.py:386
  352.7 3.5 convert_bitcast_fusion.5
  356.2 4.0 copy.180
  360.2 74.9 %all_to_all.143 = bf16[12,768,128]{2,0,1:T(8,128)(2,1)S(1)} all-to-all(bf16[12,768,128]{2,0,1:T(8,128)(2,1)S(1)} %copy.180), channel_id=1, replica_groups=mesh['lat'=8,'lon'=4] {'lon'}, dimensions={1} | all-to-all | bytes 4718592 | tf_op jit(solution)/shard_map/all_to_all | solution.py:394
  436.6 1.3 copy-done.6
  438.7 9.3 multiply_convert_fusion
  448.0 15.9 %fusion.6 = bf16[9216,512]{1,0:T(8,128)(2,1)S(1)} fusion(f32[9216,512]{1,0:T(8,128)} %get-tuple-element.50, bf16[9216,128]{1,0:T(8,128)(2,1)S(1)} %bitcast.196, bf16[512,128]{1,0:T(8,128)(2,1)S(1)} %copy-done.9), kind=kOutput, calls=%fused_computation.8 | convolution fusion | flops 1302331392 | bytes 30801920 | tf_op jit(solution)/shard_map/tc,fc->tf/dot_general | solution.py:414
  463.9 2.1 fusion.62
  466.1 2.8 fusion.7
  468.9 4.2 fusion.8
  473.1 3.4 fusion.63
  476.5 55.9 %all_to_all.144 = bf16[48,192,128]{2,1,0:T(8,128)(2,1)S(1)} all-to-all(bf16[48,192,128]{2,1,0:T(8,128)(2,1)S(1)} %bitcast.169), channel_id=1, replica_groups=mesh['lat'=8,'lon'=4] {'lon'}, dimensions={0} | all-to-all | bytes 4718592 | tf_op jit(solution)/shard_map/all_to_all | solution.py:361
  533.6 3.5 convert_bitcast_fusion.4
  537.1 5.0 copy.185
  542.1 72.8 %all_to_all.145 = bf16[12,768,128]{2,0,1:T(8,128)(2,1)S(1)} all-to-all(bf16[12,768,128]{2,0,1:T(8,128)(2,1)} %copy.185), channel_id=1, replica_groups=mesh['lat'=8,'lon'=4] {'lat','lon'}, dimensions={1} | all-to-all | bytes 4718592 | tf_op jit(solution)/shard_map/all_to_all | solution.py:365
  614.8 2.0 copy.187
  616.8 5.0 reshape.537
  621.8 6.7 convert_bitcast_fusion.3
  628.6 4.3 copy.189
  632.8 2.1 copy.190
  634.9 33.3 %all_to_all.146 = bf16[8,48,24,128]{3,1,2,0:T(8,128)(2,1)S(1)} all-to-all(bf16[8,48,24,128]{3,1,2,0:T(8,128)(2,1)S(1)} %copy.190), channel_id=1, replica_groups=mesh['lat'=8,'lon'=4] {'lat'}, dimensions={0} | all-to-all | bytes 4718592 | tf_op jit(solution)/shard_map/all_to_all | solution.py:371
  668.7 1.4 copy-done.4
  671.0 1.4 convolution_bitcast_fusion.1
  675.0 31.9 %all_to_all.147 = bf16[8,48,24,128]{3,1,2,0:T(8,128)(2,1)S(1)} all-to-all(bf16[8,48,24,128]{3,1,2,0:T(8,128)(2,1)S(1)} %bitcast.186), channel_id=1, replica_groups=mesh['lat'=8,'lon'=4] {'lat'}, dimensions={0} | all-to-all | bytes 4718592 | tf_op jit(solution)/shard_map/all_to_all | solution.py:380
  707.5 1.3 copy-done.2
  708.9 3.1 fusion.26
  712.0 4.3 copy.198
  716.2 4.6 copy.199
  720.8 3.5 all-to-all-start.10
  724.6 4.2 convolution_bitcast_fusion
  730.1 2.0 pad_maximum_fusion
  732.0 4.9 copy.210
  737.0 83.5 %all-to-all-done.10 = bf16[384,24,128]{2,1,0:T(8,128)(2,1)} async-done(((bf16[384,24,128]{2,1,0:T(8,128)(2,1)}), bf16[384,24,128]{2,1,0:T(8,128)(2,1)}, u32[]{:S(2)}, u32[]{:S(2)}) %all-to-all-start.10) | async-done | bytes 2359328 | tf_op jit(solution)/shard_map/all_to_all | solution.py:386
  820.5 2.3 copy.200
  822.8 3.5 convert_bitcast_fusion.2
  826.3 5.0 copy.203
  831.3 5.5 all-to-all-start.11
  837.5 2.9 copy.211
  840.4 70.9 %all-to-all-done.11 = bf16[12,768,128]{2,0,1:T(8,128)(2,1)} async-done(((bf16[12,768,128]{2,0,1:T(8,128)(2,1)}), bf16[12,768,128]{2,0,1:T(8,128)(2,1)}, u32[]{:S(2)}, u32[]{:S(2)}) %all-to-all-start.11) | async-done | bytes 2359328 | tf_op jit(solution)/shard_map/all_to_all | solution.py:394
  911.3 2.5 copy.204
  914.7 2.2 fusion.9
  916.8 96.4 %all-reduce.4.cloned.1.call-done = (f32[128,512]{1,0:T(8,128)}, f32[512,128]{1,0:T(8,128)}) async-done(((f32[128,512]{1,0:T(8,128)}, f32[512,128]{1,0:T(8,128)}), (f32[128,512]{1,0:T(8,128)}, f32[512,128]{1,0:T(8,128)})) %all-reduce.4.cloned.1.call-update) | async-done | bytes 524304 | tf_op jit(solution)/shard_map/psum | solution.py:424
  1013.3 1.7 copy.266
  1014.9 1.7 copy.267
  (75 shorter events, 18.9 us)
Async XLA Ops:
  7.2 431.5 %copy-start = (bf16[128,512]{1,0:T(8,128)(2,1)S(1)}, bf16[128,512]{1,0:T(8,128)(2,1)}, u32[]{:S(2)}) copy-start(bf16[128,512]{1,0:T(8,128)(2,1)} %param.14) | copy-start | bytes 393220
  7.2 60.3 %all-to-all-start = ((bf16[48,192,128]{2,1,0:T(8,128)(2,1)}), bf16[48,192,128]{2,1,0:T(8,128)(2,1)S(1)}, u32[]{:S(2)}, u32[]{:S(2)}) async-start(bf16[48,192,128]{2,1,0:T(8,128)(2,1)} %param.11), calls=%async_computation | async-start | bytes 4718592 | tf_op jit(solution)/shard_map/all_to_all | solution.py:361
  67.5 1.3 copy-start.13
  74.0 123.1 %all-to-all-start.1 = ((bf16[12,768,128]{2,0,1:T(8,128)(2,1)}), bf16[12,768,128]{2,0,1:T(8,128)(2,1)S(1)}, u32[]{:S(2)}, u32[]{:S(2)}) async-start(bf16[12,768,128]{2,0,1:T(8,128)(2,1)} %copy.163), calls=%async_computation.1 | async-start | bytes 6291456 | tf_op jit(solution)/shard_map/all_to_all | solution.py:365
  77.7 2.5 copy-start.11
  77.7 2.7 copy-start.10
  77.7 167.9 %all-gather.2.cloned.1.call-start = ((), (), s32[]{:S(2)}) async-start(), calls=%async_computation.13 | async-start | bytes 3932160 | tf_op jit(solution)/shard_map/all_gather | solution.py:358
  80.5 6.7 copy-start.12
  245.6 4.2 copy-start.3
  284.3 2.0 copy-start.1
  351.4 1.3 copy-start.15
  436.3 1.7 copy-start.6
  438.7 9.3 copy-start.7
  438.7 9.3 copy-start.9
  463.9 2.2 copy-start.8
  532.4 1.3 copy-start.16
  668.3 2.7 copy-start.5
  668.7 1.4 copy-start.4
  706.9 2.0 copy-start.2
  706.9 2.0 copy-start.17
  720.8 99.6 %all-to-all-start.10 = ((bf16[384,24,128]{2,1,0:T(8,128)(2,1)}), bf16[384,24,128]{2,1,0:T(8,128)(2,1)}, u32[]{:S(2)}, u32[]{:S(2)}) async-start(bf16[384,24,128]{2,1,0:T(8,128)(2,1)} %copy.199), calls=%async_computation.10 | async-start | bytes 4718592 | tf_op jit(solution)/shard_map/all_to_all | solution.py:386
  724.3 113.2 %reduce-scatter.2.cloned.1.call-start = ((), (), s32[]{:S(2)}) async-start(), calls=%async_computation.14 | async-start | bytes 3932160 | tf_op jit(solution)/shard_map/reduce_scatter | solution.py:426
  820.5 2.3 copy-start.14
  831.3 80.0 %all-to-all-start.11 = ((bf16[12,768,128]{2,0,1:T(8,128)(2,1)}), bf16[12,768,128]{2,0,1:T(8,128)(2,1)}, u32[]{:S(2)}, u32[]{:S(2)}) async-start(bf16[12,768,128]{2,0,1:T(8,128)(2,1)} %copy.203), calls=%async_computation.11 | async-start | bytes 6291456 | tf_op jit(solution)/shard_map/all_to_all | solution.py:394
  836.8 176.5 %all-reduce.4.cloned.1.call-start = ((), (), s32[]{:S(2)}) async-start(), calls=%async_computation.15 | async-start | bytes 1048576 | tf_op jit(solution)/shard_map/psum | solution.py:424
Sparse Core Ops, SparseCore 0:
  80.7 116.3 all-gather.1
  737.1 87.4 reduce-scatter.1
  843.7 169.5 all-reduce.3

commit v2 on v1

--- a/solution.py
+++ b/solution.py
@@ -328,6 +328,28 @@
     )
 
 
+def shift_exchange(values, split_axis, concat_axis):
+    devices = lax.axis_size("lon")
+    place = lax.axis_index("lon")
+    split = values.shape[split_axis] // devices
+    extent = values.shape[concat_axis]
+    shape = list(values.shape)
+    shape[split_axis] = split
+    shape[concat_axis] = extent * devices
+    gathered = jnp.zeros(shape, values.dtype)
+    for shift in range(devices):
+        target = (place + shift) % devices
+        source = (place + devices - shift) % devices
+        block = lax.dynamic_slice_in_dim(values, target * split, split, axis=split_axis)
+        if shift:
+            pairs = [(index, (index + shift) % devices) for index in range(devices)]
+            block = lax.ppermute(block, "lon", pairs)
+        gathered = lax.dynamic_update_slice_in_dim(
+            gathered, block, source * extent, axis=concat_axis
+        )
+    return gathered
+
+
 def on_device(grid_state, upstream, spectral_weight, up_weight, down_weight):
     lat_devices = lax.axis_size("lat")
     lon_devices = lax.axis_size("lon")
@@ -357,23 +379,25 @@
     table = order_table(order_ids, degrees, cosines, log_sines)
     weight = lax.all_gather(spectral_weight, "lon", axis=0, tiled=True)
 
-    def grid_to_degrees(values, fourier, scale):
-        circles = lax.all_to_all(values, "lon", split_axis=0, concat_axis=1, tiled=True)
+    def grid_to_degrees(circles, fourier, scale, waiting):
         spectrum = jnp.einsum("jnc,nq->jqc", circles, fourier, preferred_element_type=jnp.float32)
         if scale is not None:
             spectrum = spectrum * scale[:, None, None]
         spectrum = lax.all_to_all(
             spectrum.astype(jnp.bfloat16), both, split_axis=1, concat_axis=0, tiled=True
-        ).reshape(degrees, 2, orders, channels)
+        )
+        spectrum, waiting = lax.optimization_barrier((spectrum, waiting))
+        spectrum = spectrum.reshape(degrees, 2, orders, channels)
         coeffs = jnp.einsum(
             "mlj,jrmc->lrmc", table, spectrum, preferred_element_type=jnp.float32
         ).astype(jnp.bfloat16)
         coeffs = lax.all_to_all(
             coeffs.reshape(lat_devices, lat_rows, 2 * orders, channels), "lat", 0, 0, tiled=True
         ).reshape(lat_devices, lat_rows, 2, orders, channels)
-        return coeffs.transpose(1, 2, 0, 3, 4).reshape(
+        coeffs = coeffs.transpose(1, 2, 0, 3, 4).reshape(
             lat_rows, 2, lat_devices * orders, channels
         )
+        return (coeffs, waiting)
 
     def degrees_to_grid(coeffs, fourier, scale):
         coeffs = coeffs.reshape(lat_rows, 2, lat_devices, orders, channels).transpose(2, 0, 1, 3, 4)
@@ -391,14 +415,14 @@
             tiled=True,
         )
         circles = jnp.einsum("jqc,nq->jnc", spectrum, fourier, preferred_element_type=jnp.float32)
-        return lax.all_to_all(
-            circles.astype(jnp.bfloat16), "lon", split_axis=1, concat_axis=0, tiled=True
-        )
-
-    coeffs = grid_to_degrees(grid_state, fourier_fwd, quad_own)
+        return circles.astype(jnp.bfloat16)
+
+    state = lax.all_to_all(grid_state, "lon", split_axis=0, concat_axis=1, tiled=True)
+    coeffs, upstream = grid_to_degrees(state, fourier_fwd, quad_own, upstream)
+    upstream = shift_exchange(upstream, 0, 1)
     mixed_coeffs = forward_mix(coeffs, weight).astype(jnp.bfloat16)
     spectral_part = degrees_to_grid(mixed_coeffs, fourier_inv, None)
-    mid_state = (grid_state.astype(jnp.float32) + spectral_part.astype(jnp.float32)).astype(
+    mid_state = (state.astype(jnp.float32) + spectral_part.astype(jnp.float32)).astype(
         jnp.bfloat16
     )
     mid_rows = mid_state.reshape(-1, channels)
@@ -408,7 +432,7 @@
     next_rows = mid_rows.astype(jnp.float32) + jnp.dot(
         activation, down_weight, preferred_element_type=jnp.float32
     )
-    next_state = next_rows.astype(jnp.bfloat16).reshape(lat_rows, lon_cells, channels)
+    next_state = next_rows.astype(jnp.bfloat16).reshape(cycles, lon_total, channels)
     up_rows = upstream.reshape(-1, channels)
     down_part = jnp.einsum("tf,tc->fc", activation, up_rows, preferred_element_type=jnp.float32)
     pulled = jnp.einsum("tc,fc->tf", up_rows, down_weight, preferred_element_type=jnp.float32)
@@ -417,12 +441,14 @@
     grad_mid = up_rows.astype(jnp.float32) + jnp.einsum(
         "tf,cf->tc", grad_hidden, up_weight, preferred_element_type=jnp.float32
     )
-    grad_mid = grad_mid.astype(jnp.bfloat16).reshape(lat_rows, lon_cells, channels)
+    grad_mid = grad_mid.astype(jnp.bfloat16).reshape(cycles, lon_total, channels)
     grad_mid, up_part, down_part, next_state = lax.optimization_barrier(
         (grad_mid, up_part, down_part, next_state)
     )
     grad_up, grad_down = lax.psum((up_part, down_part), both)
-    grad_mixed = grid_to_degrees(grad_mid, fourier_inv, None)
+    grad_mixed, next_state = grid_to_degrees(grad_mid, fourier_inv, None, next_state)
+    next_state = shift_exchange(next_state, 1, 0)
+    grad_mixed, grad_up, grad_down = lax.optimization_barrier((grad_mixed, grad_up, grad_down))
     grad_spectral = lax.psum_scatter(
         weight_grad(coeffs, grad_mixed).astype(jnp.bfloat16), "lon", scatter_dimension=0, tiled=True
     ).astype(jnp.float32)
@@ -431,6 +457,7 @@
     grad_state = (grad_mid.astype(jnp.float32) + grad_spectral_part.astype(jnp.float32)).astype(
         jnp.bfloat16
     )
+    grad_state = lax.all_to_all(grad_state, "lon", split_axis=1, concat_axis=0, tiled=True)
     return (next_state, grad_state, grad_spectral, grad_up, grad_down)
 
 

time: 1030 us -> 1010 us (0.981)
  blocking collectives: 391 us -> 183 us
  waiting for transfers between devices: 396 us -> 545 us
  starting transfers between devices: 19.5 us -> 39.6 us
  local copies, waits for them, and re-layouts: 88.3 us -> 107 us
    all_to_all x3 -> x0, blocking collectives: 188 us -> none  [the longest x1 74.9 us: degrees_to_grid(): lax.all_to_all(circles.astype(jnp.bfloat16), 'lon', split_axis=1, concat_...]
    ppermute x0 -> x6, waiting for transfers between devices: none -> 182 us  [shift_exchange(): block = lax.ppermute(block, 'lon', pairs)]
    all_to_all x2 -> x3, waiting for transfers between devices: 124 us -> 82.8 us  [the longest x1 53.1 us: on_device(): lax.all_to_all(grid_state, 'lon', split_axis=0, concat_axis=1, tiled=True)]
    all_to_all x2 -> x1, blocking collectives: 66.6 us -> 33.2 us  [grid_to_degrees(): lax.all_to_all(coeffs.reshape(lat_devices, lat_rows, 2 * orders, channels...]
    all_to_all x1, blocking collectives: 72.8 us -> 85.6 us  [grid_to_degrees(): lax.all_to_all(spectrum.astype(jnp.bfloat16), both, split_axis=1, concat_...]
    ppermute x0 -> x6, starting transfers between devices: none -> 11.8 us  [shift_exchange(): block = lax.ppermute(block, 'lon', pairs)]
    psum x1, waiting for transfers between devices: 96.4 us -> 107 us  [on_device(): grad_up, grad_down = lax.psum((up_part, down_part), both)]
    all_to_all x1 -> x2, waiting for transfers between devices: 83.5 us -> 80.1 us  [degrees_to_grid(): lax.all_to_all(spectrum.astype(jnp.bfloat16).reshape(degrees, 2 * orders,...]
  transfers between devices with their start and end apart: 7 -> 15, of which waited for: 5 -> 9; matrix products, arithmetic and copies ran while one was open for 6% -> 7% of each run, Pallas kernels for 2% -> 2%
where the time goes in v2:
time: 1010 us; the launch traced here: 999 us
  waiting for transfers between devices  545 us (54%)
  blocking collectives  183 us (18%)
  local copies, waits for them, and re-layouts  107 us (11%)
  matrix products  78.9 us (8%)
  starting transfers between devices  39.6 us (4%)
  Pallas kernels  18.3 us (2%)
  between operations  14.5 us (1%)
  other arithmetic  12.7 us (1%)
    ppermute x6, waiting for transfers between devices, shift_exchange(): block = lax.ppermute(block, 'lon', pairs)  182 us
    psum x1, waiting for transfers between devices, on_device(): grad_up, grad_down = lax.psum((up_part, down_part), both)  107 us
    all_to_all x1, waiting for transfers between devices, grid_to_degrees(): lax.all_to_all(spectrum.astype(jnp.bfloat16), both, split_axis=1, concat_...  92.8 us
    all_to_all x1, blocking collectives, grid_to_degrees(): lax.all_to_all(spectrum.astype(jnp.bfloat16), both, split_axis=1, concat_...  85.6 us
    all_to_all x2, waiting for transfers between devices, degrees_to_grid(): lax.all_to_all(spectrum.astype(jnp.bfloat16).reshape(degrees, 2 * orders,...  80.1 us
    all_to_all x2, blocking collectives, degrees_to_grid(): lax.all_to_all(coeffs.reshape(lat_devices, lat_rows, 2 * orders, channels...  64.7 us
    all_to_all x1, waiting for transfers between devices, on_device(): lax.all_to_all(grid_state, 'lon', split_axis=0, concat_axis=1, tiled=True)  53.1 us
    all_to_all x1, blocking collectives, grid_to_degrees(): lax.all_to_all(coeffs.reshape(lat_devices, lat_rows, 2 * orders, channels...  33.2 us
  transfers between devices with their start and end apart: 15, of which 9 were waited for; matrix products, arithmetic and copies ran while one was open for 7% of the time, Pallas kernels for 2%

profile of v2, /device:TPU:0, one launch (start us, length us, event | category | flops | bytes accessed | tf_op | source)
XLA Modules:
  0.0 998.9 jit_solution(15213455339290402508)
XLA Ops:
  7.2 6.5 all-to-all-start
  14.4 53.1 %all-to-all-done = bf16[48,192,128]{2,1,0:T(8,128)(2,1)S(1)} async-done(((bf16[48,192,128]{2,1,0:T(8,128)(2,1)}), bf16[48,192,128]{2,1,0:T(8,128)(2,1)S(1)}, u32[]{:S(2)}, u32[]{:S(2)}) %all-to-all-start) | async-done | bytes 2359328 | tf_op jit(solution)/shard_map/all_to_all | solution.py:420
  69.1 2.0 fusion.24
  71.1 3.3 copy.218
  74.4 3.8 all-to-all-start.1
  79.8 6.7 sqrt_multiply_fusion
  86.5 18.3 %shard_map.146 = bf16[12,384,384]{2,1,0:T(8,128)(2,1)} custom-call(f32[16,384]{1,0:T(8,128)S(1)} %broadcast_in_dim.28.refs_0_, f32[16,384]{1,0:T(8,128)S(1)} %multiply_add_fusion.refs_1_, f32[384,16,1]{2,1,0:T(8,128)S(1)} %get-tuple-element.72.refs_2_, f32[384,16,1]{2,1,0:T(8,128)} %get-tuple-element.71.refs_3_, f32[384,16,1]{2,1,0:T(8,128)} %get-tuple-element.73.refs_4_), custom_call_target="tpu_custom_call" | custom-call | flops 28311552 | bytes 3538944 | tf_op jit(solution)/shard_map/pallas_call | solution.py:310
  104.8 92.8 %all-to-all-done.1 = bf16[12,768,128]{2,0,1:T(8,128)(2,1)} async-done(((bf16[12,768,128]{2,0,1:T(8,128)(2,1)}), bf16[12,768,128]{2,0,1:T(8,128)(2,1)}, u32[]{:S(2)}, u32[]{:S(2)}) %all-to-all-start.1) | async-done | bytes 2359328 | tf_op jit(solution)/shard_map/all_to_all | solution.py:386
  197.6 2.5 copy.220
  202.1 3.3 convert_bitcast_fusion.3
  205.4 3.2 copy.223
  209.0 33.2 %all_to_all.128 = bf16[8,48,24,128]{3,1,2,0:T(8,128)(2,1)S(1)} all-to-all(bf16[8,48,24,128]{3,1,2,0:T(8,128)(2,1)S(1)} %copy.224), channel_id=1, replica_groups=mesh['lat'=8,'lon'=4] {'lat'}, dimensions={0} | all-to-all | bytes 4718592 | tf_op jit(solution)/shard_map/all_to_all | solution.py:394
  242.7 3.3 convolution_bitcast_fusion.2
  248.6 31.9 %all_to_all.129 = bf16[8,48,24,128]{3,1,2,0:T(8,128)(2,1)S(1)} all-to-all(bf16[8,48,24,128]{3,1,2,0:T(8,128)(2,1)S(1)} %bitcast.167), channel_id=1, replica_groups=mesh['lat'=8,'lon'=4] {'lat'}, dimensions={0} | all-to-all | bytes 4718592 | tf_op jit(solution)/shard_map/all_to_all | solution.py:404
  282.5 3.1 convert_bitcast_fusion.2
  285.5 4.3 copy.233
  289.8 4.6 copy.234
  294.4 3.5 all-to-all-start.4
  302.0 2.6 collective-permute-start
  307.7 46.2 %collective-permute-done = bf16[12,192,128]{2,1,0:T(8,128)(2,1)} collective-permute-done((bf16[12,192,128]{2,1,0:T(8,128)(2,1)}, bf16[12,192,128]{2,1,0:T(8,128)(2,1)}, u32[]{:S(2)}, u32[]{:S(2)}) %collective-permute-start) | collective-permute-done | bytes 589856 | tf_op jit(solution)/shard_map/ppermute | solution.py:346
  354.0 2.0 constant_dynamic-update-slice_fusion.5
  356.0 35.0 %collective-permute-done.1 = bf16[12,192,128]{2,1,0:T(8,128)(2,1)} collective-permute-done((bf16[12,192,128]{2,1,0:T(8,128)(2,1)}, bf16[12,192,128]{2,1,0:T(8,128)(2,1)}, u32[]{:S(2)}, u32[]{:S(2)}) %collective-permute-start.1) | collective-permute-done | bytes 589856 | tf_op jit(solution)/shard_map/ppermute | solution.py:346
  391.0 2.0 constant_dynamic-update-slice_fusion.4
  393.0 2.0 constant_dynamic-update-slice_fusion.3
  395.0 2.4 copy.235
  397.7 2.0 fusion.9
  399.7 9.3 multiply_convert_fusion
  409.1 3.8 fusion.7
  412.9 5.0 fusion.62
  417.9 17.2 %fusion.6 = bf16[9216,512]{1,0:T(8,128)(2,1)S(1)} fusion(f32[9216,512]{1,0:T(8,128)} %get-tuple-element.77, bf16[9216,128]{1,0:T(8,128)(2,1)} %bitcast.9, bf16[512,128]{1,0:T(8,128)(2,1)S(1)} %copy-done.18), kind=kOutput, calls=%fused_computation.8 | convolution fusion | flops 1302331392 | bytes 30801920 | tf_op jit(solution)/shard_map/tc,fc->tf/dot_general | solution.py:438
  435.1 3.6 copy-done.1
  438.7 2.1 fusion.61
  440.9 7.1 add_convert_fusion
  449.4 3.5 convert_bitcast_fusion.1
  452.8 5.0 copy.239
  457.8 85.6 %all_to_all.130 = bf16[12,768,128]{2,0,1:T(8,128)(2,1)S(1)} all-to-all(bf16[12,768,128]{2,0,1:T(8,128)(2,1)} %copy.239), channel_id=1, replica_groups=mesh['lat'=8,'lon'=4] {'lat','lon'}, dimensions={1} | all-to-all | bytes 4718592 | tf_op jit(solution)/shard_map/all_to_all | solution.py:386
  546.0 3.3 convert_bitcast_fusion
  549.3 4.3 copy.245
  553.5 3.5 copy.246
  557.0 4.4 all-to-all-start.6
  562.2 29.7 %all-to-all-done.6 = bf16[8,48,24,128]{3,1,2,0:T(8,128)(2,1)} async-done(((bf16[8,48,24,128]{3,1,2,0:T(8,128)(2,1)}), bf16[8,48,24,128]{3,1,2,0:T(8,128)(2,1)}, u32[]{:S(2)}, u32[]{:S(2)}) %all-to-all-start.6) | async-done | bytes 2359328 | tf_op jit(solution)/shard_map/all_to_all | solution.py:394
  591.9 3.5 copy.247
  595.4 106.8 %all-reduce.4.cloned.1.call-done = (f32[128,512]{1,0:T(8,128)}, f32[512,128]{1,0:T(8,128)}) async-done(((f32[128,512]{1,0:T(8,128)}, f32[512,128]{1,0:T(8,128)}), (f32[128,512]{1,0:T(8,128)}, f32[512,128]{1,0:T(8,128)})) %all-reduce.4.cloned.1.call-update) | async-done | bytes 524304 | tf_op jit(solution)/shard_map/psum | solution.py:448
  702.2 4.0 convolution_bitcast_fusion.1
  708.8 32.8 %all_to_all.131 = bf16[8,48,24,128]{3,1,2,0:T(8,128)(2,1)S(1)} all-to-all(bf16[8,48,24,128]{3,1,2,0:T(8,128)(2,1)S(1)} %bitcast.170), channel_id=1, replica_groups=mesh['lat'=8,'lon'=4] {'lat'}, dimensions={0} | all-to-all | bytes 4718592 | tf_op jit(solution)/shard_map/all_to_all | solution.py:404
  743.6 3.1 fusion.25
  746.7 4.3 copy.254
  750.9 4.7 copy.255
  755.6 3.5 all-to-all-start.8
  759.4 3.5 convolution_bitcast_fusion
  764.1 1.9 pad_maximum_fusion
  766.1 4.9 copy.266
  772.7 2.4 copy.242
  775.1 80.1 %all-to-all-done.8 = bf16[384,24,128]{2,1,0:T(8,128)(2,1)} async-done(((bf16[384,24,128]{2,1,0:T(8,128)(2,1)}), bf16[384,24,128]{2,1,0:T(8,128)(2,1)}, u32[]{:S(2)}, u32[]{:S(2)}) %all-to-all-start.8) | async-done | bytes 2359328 | tf_op jit(solution)/shard_map/all_to_all | solution.py:410
  855.2 2.4 copy.256
  857.9 3.5 fusion.8
  861.4 5.0 copy.259
  866.4 5.6 all-to-all-start.9
  872.0 2.0 broadcast_in_dim.24
  875.0 3.4 collective-permute-start.3
  881.1 59.8 %collective-permute-done.3 = bf16[12,192,128]{2,1,0:T(8,128)(2,1)S(1)} collective-permute-done((bf16[12,192,128]{2,1,0:T(8,128)(2,1)S(1)}, bf16[12,192,128]{2,1,0:T(8,128)(2,1)S(1)}, u32[]{:S(2)}, u32[]{:S(2)}) %collective-permute-start.3) | collective-permute-done | bytes 589856 | tf_op jit(solution)/shard_map/ppermute | solution.py:346
  941.8 40.4 %collective-permute-done.4 = bf16[12,192,128]{2,1,0:T(8,128)(2,1)S(1)} collective-permute-done((bf16[12,192,128]{2,1,0:T(8,128)(2,1)S(1)}, bf16[12,192,128]{2,1,0:T(8,128)(2,1)S(1)}, u32[]{:S(2)}, u32[]{:S(2)}) %collective-permute-start.4) | collective-permute-done | bytes 589856 | tf_op jit(solution)/shard_map/ppermute | solution.py:346
  983.9 2.9 copy.267
  986.8 4.0 copy.261
  (103 shorter events, 39.2 us)
Async XLA Ops:
  7.2 392.6 %copy-start = (bf16[128,512]{1,0:T(8,128)(2,1)S(1)}, bf16[128,512]{1,0:T(8,128)(2,1)}, u32[]{:S(2)}) copy-start(bf16[128,512]{1,0:T(8,128)(2,1)} %param.14) | copy-start | bytes 393220
  7.2 60.3 %all-to-all-start = ((bf16[48,192,128]{2,1,0:T(8,128)(2,1)}), bf16[48,192,128]{2,1,0:T(8,128)(2,1)S(1)}, u32[]{:S(2)}, u32[]{:S(2)}) async-start(bf16[48,192,128]{2,1,0:T(8,128)(2,1)} %param.11), calls=%async_computation | async-start | bytes 4718592 | tf_op jit(solution)/shard_map/all_to_all | solution.py:420
  67.5 1.6 copy-start.13
  67.7 1.4 copy-start.11
  74.4 3.9 copy-start.15
  74.4 123.2 %all-to-all-start.1 = ((bf16[12,768,128]{2,0,1:T(8,128)(2,1)}), bf16[12,768,128]{2,0,1:T(8,128)(2,1)}, u32[]{:S(2)}, u32[]{:S(2)}) async-start(bf16[12,768,128]{2,0,1:T(8,128)(2,1)} %copy.218), calls=%async_computation.1 | async-start | bytes 6291456 | tf_op jit(solution)/shard_map/all_to_all | solution.py:386
  78.2 1.4 copy-start.20
  78.2 1.5 copy-start.19
  78.2 164.5 %all-gather.2.cloned.1.call-start = ((), (), s32[]{:S(2)}) async-start(), calls=%async_computation.11 | async-start | bytes 3932160 | tf_op jit(solution)/shard_map/all_gather | solution.py:380
  79.8 6.7 copy-start.21
  200.1 2.0 copy-start.2
  280.5 2.0 copy-start.3
  294.4 100.6 %all-to-all-start.4 = ((bf16[384,24,128]{2,1,0:T(8,128)(2,1)}), bf16[384,24,128]{2,1,0:T(8,128)(2,1)}, u32[]{:S(2)}, u32[]{:S(2)}) async-start(bf16[384,24,128]{2,1,0:T(8,128)(2,1)} %copy.234), calls=%async_computation.4 | async-start | bytes 4718592 | tf_op jit(solution)/shard_map/all_to_all | solution.py:410
  298.0 2.4 copy-start.10
  302.0 51.9 %collective-permute-start = (bf16[12,192,128]{2,1,0:T(8,128)(2,1)}, bf16[12,192,128]{2,1,0:T(8,128)(2,1)}, u32[]{:S(2)}, u32[]{:S(2)}) collective-permute-start(bf16[12,192,128]{2,1,0:T(8,128)(2,1)} %get-tuple-element.69), channel_id=1, source_target_pairs={{0,1},{1,2},{2,3},{3,0},{4,5},{5,6},{6,7},{7,4},{8,9},{9,10},{10,1... | collective-permute-start | bytes 1769480 | tf_op jit(solution)/shard_map/ppermute | solution.py:346
  304.6 86.4 %collective-permute-start.1 = (bf16[12,192,128]{2,1,0:T(8,128)(2,1)}, bf16[12,192,128]{2,1,0:T(8,128)(2,1)}, u32[]{:S(2)}, u32[]{:S(2)}) collective-permute-start(bf16[12,192,128]{2,1,0:T(8,128)(2,1)} %get-tuple-element.68), channel_id=1, source_target_pairs={{0,2},{1,3},{2,0},{3,1},{4,6},{5,7},{6,4},{7,5},{8,10},{9,11},{10,... | collective-permute-start | bytes 1769480 | tf_op jit(solution)/shard_map/ppermute | solution.py:346
  306.1 86.9 %collective-permute-start.2 = (bf16[12,192,128]{2,1,0:T(8,128)(2,1)S(1)}, bf16[12,192,128]{2,1,0:T(8,128)(2,1)}, u32[]{:S(2)}, u32[]{:S(2)}) collective-permute-start(bf16[12,192,128]{2,1,0:T(8,128)(2,1)S(1)} %get-tuple-element.67), channel_id=1, source_target_pairs={{0,3},{1,0},{2,1},{3,2},{4,7},{5,4},{6,5},{7,6},{8,11},{9,8},{10,9... | collective-permute-start | bytes 1769480 | tf_op jit(solution)/shard_map/ppermute | solution.py:346
  395.0 2.4 copy-start.12
  395.0 2.7 copy-start.22
  399.7 9.3 copy-start.18
  435.1 3.6 copy-start.1
  440.9 8.5 copy-start.23
  447.9 1.4 copy-start.7
  544.0 2.0 copy-start.4
  557.0 34.9 %all-to-all-start.6 = ((bf16[8,48,24,128]{3,1,2,0:T(8,128)(2,1)}), bf16[8,48,24,128]{3,1,2,0:T(8,128)(2,1)}, u32[]{:S(2)}, u32[]{:S(2)}) async-start(bf16[8,48,24,128]{3,1,2,0:T(8,128)(2,1)} %copy.246), calls=%async_computation.6 | async-start | bytes 4718592 | tf_op jit(solution)/shard_map/all_to_all | solution.py:394
  561.4 140.8 %all-reduce.4.cloned.1.call-start = ((), (), s32[]{:S(2)}) async-start(), calls=%async_computation.13 | async-start | bytes 1048576 | tf_op jit(solution)/shard_map/psum | solution.py:448
  741.6 2.0 copy-start.5
  741.6 2.0 copy-start.24
  755.6 99.6 %all-to-all-start.8 = ((bf16[384,24,128]{2,1,0:T(8,128)(2,1)}), bf16[384,24,128]{2,1,0:T(8,128)(2,1)}, u32[]{:S(2)}, u32[]{:S(2)}) async-start(bf16[384,24,128]{2,1,0:T(8,128)(2,1)} %copy.255), calls=%async_computation.8 | async-start | bytes 4718592 | tf_op jit(solution)/shard_map/all_to_all | solution.py:410
  759.1 224.8 %reduce-scatter.2.cloned.1.call-start = ((), (), s32[]{:S(2)}) async-start(), calls=%async_computation.12 | async-start | bytes 3932160 | tf_op jit(solution)/shard_map/reduce_scatter | solution.py:452
  771.0 1.7 copy-start.8
  855.2 2.4 copy-start.9
  855.2 2.7 copy-start.14
  866.4 120.4 %all-to-all-start.9 = ((bf16[12,768,128]{2,0,1:T(8,128)(2,1)}), bf16[12,768,128]{2,0,1:T(8,128)(2,1)}, u32[]{:S(2)}, u32[]{:S(2)}) async-start(bf16[12,768,128]{2,0,1:T(8,128)(2,1)} %copy.259), calls=%async_computation.9 | async-start | bytes 6291456 | tf_op jit(solution)/shard_map/all_to_all | solution.py:460
  872.0 2.0 copy-start.6
  875.0 65.9 %collective-permute-start.3 = (bf16[12,192,128]{2,1,0:T(8,128)(2,1)S(1)}, bf16[12,192,128]{2,1,0:T(8,128)(2,1)S(1)}, u32[]{:S(2)}, u32[]{:S(2)}) collective-permute-start(bf16[12,192,128]{2,1,0:T(8,128)(2,1)S(1)} %get-tuple-element.65), channel_id=1, source_target_pairs={{0,1},{1,2},{2,3},{3,0},{4,5},{5,6},{6,7},{7,4},{8,9},{9,10},{10,1... | collective-permute-start | bytes 1769480 | tf_op jit(solution)/shard_map/ppermute | solution.py:346
  878.4 103.8 %collective-permute-start.4 = (bf16[12,192,128]{2,1,0:T(8,128)(2,1)S(1)}, bf16[12,192,128]{2,1,0:T(8,128)(2,1)S(1)}, u32[]{:S(2)}, u32[]{:S(2)}) collective-permute-start(bf16[12,192,128]{2,1,0:T(8,128)(2,1)S(1)} %get-tuple-element.64), channel_id=1, source_target_pairs={{0,2},{1,3},{2,0},{3,1},{4,6},{5,7},{6,4},{7,5},{8,10},{9,11},{10,... | collective-permute-start | bytes 1769480 | tf_op jit(solution)/shard_map/ppermute | solution.py:346
  879.3 103.7 %collective-permute-start.5 = (bf16[12,192,128]{2,1,0:T(8,128)(2,1)S(1)}, bf16[12,192,128]{2,1,0:T(8,128)(2,1)S(1)}, u32[]{:S(2)}, u32[]{:S(2)}) collective-permute-start(bf16[12,192,128]{2,1,0:T(8,128)(2,1)S(1)} %get-tuple-element.63), channel_id=1, source_target_pairs={{0,3},{1,0},{2,1},{3,2},{4,7},{5,4},{6,5},{7,6},{8,11},{9,8},{10,9... | collective-permute-start | bytes 1769480 | tf_op jit(solution)/shard_map/ppermute | solution.py:346
  986.8 4.0 copy-start.17
  986.8 4.7 copy-start.16
Sparse Core Ops, SparseCore 0:
  81.2 116.2 all-gather.1
  568.3 133.8 all-reduce.3
  771.2 88.0 reduce-scatter.1
